TPU v7x, 256 devices: a whole 4x4x8 slice. The times are simulated.
256 devices in a mesh: leaf: 32 (over y, x, core), lobe: 8 (over z).
Axes of the slice: x: 4, y: 4, z: 8, core: 2. Of those that a mesh axis runs over, the one named last changes fastest.
Arguments:
- base_velocity: float32 [3, 512, 65536], P(None, None, ('leaf', 'lobe')), may hold values from -6 to 6
- adjoint_velocity: float32 [3, 512, 65536], P(None, None, ('leaf', 'lobe')), may hold values from -6 to 6
- element_size: float32 [65536], P(('leaf', 'lobe')), may hold values from 0.5 to 2
- link_slot: int32 [32768], P(('leaf', 'lobe')), may hold values from -1 to 511, as said below
Outputs:
- adjoint_out: float32 [3, 512, 65536], P(None, None, ('leaf', 'lobe'))
- pressure: float32 [512, 65536], P(None, ('leaf', 'lobe'))
Inputs may be any that keep to these rules, and one draw needn't show every extreme that they name: `link_slot`: within one lobe index, row b * 4 + c of leaf index a is >= 0 exactly when row a * 4 + c of leaf index b is; rows naming the device's own leaf index are -1; every row naming leaf index a XOR 1 is >= 0. The values >= 0 of one device are distinct; each names element s % 256 and face 2 + s // 256.
All inputs are finite; a program needn't handle non-finite values.
Results may differ from a plain program's by a relative error of at most 0.0001.
Values sent between devices are 32-bit elements; how exact they have to be, the bound alone decides.
A program may use at most 128 MiB of HBM per device.

v0:
```python
import functools
import math

import jax
import jax.numpy as jnp
import numpy as np
from jax import lax
from jax.experimental import pallas as pl
from jax.experimental.pallas import tpu as pltpu
from jax.sharding import PartitionSpec as P

NP = 8
EL = 256
MODES = 104
MODES16 = 112

time_step = 0.01
viscosity = 0.002
penalty = 0.5
shift_term = 1.0

F32 = jnp.float32
BF16 = jnp.bfloat16


def legendre_columns(points, degree):
    table = np.zeros((points.shape[0], degree + 1))
    table[:, 0] = 1.0
    table[:, 1] = points
    for order in range(2, degree + 1):
        table[:, order] = (
            (2 * order - 1) * points * table[:, order - 1] - (order - 1) * table[:, order - 2]
        ) / order
    return table


def node_tables():
    degree = NP - 1
    node_points = np.cos(np.pi * np.arange(degree + 1) / degree)
    for sweep in range(100):
        table = legendre_columns(node_points, degree)
        node_points = node_points - (node_points * table[:, degree] - table[:, degree - 1]) / (
            (degree + 1) * table[:, degree]
        )
    node_points = np.sort(node_points)
    values = legendre_columns(node_points, degree)[:, degree]
    matrix = np.zeros((NP, NP))
    for row_index in range(NP):
        for col_index in range(NP):
            if row_index != col_index:
                matrix[row_index, col_index] = values[row_index] / (
                    values[col_index] * (node_points[row_index] - node_points[col_index])
                )
    matrix[0, 0] = -degree * (degree + 1) / 4.0
    matrix[-1, -1] = degree * (degree + 1) / 4.0
    return matrix


def schwarz_tables():
    grid_count = NP + 2
    mode_index = np.arange(1, grid_count + 1)
    sine_basis = math.sqrt(2.0 / (grid_count + 1)) * np.sin(
        np.pi * np.outer(mode_index, mode_index) / (grid_count + 1)
    )
    eigen_values = 2.0 - 2.0 * np.cos(np.pi * mode_index / (grid_count + 1))
    return (sine_basis, eigen_values)


def three(matrix):
    high = matrix.astype(np.float32).astype(jnp.bfloat16)
    low = (matrix - high.astype(np.float64)).astype(np.float32).astype(jnp.bfloat16)
    return np.concatenate([high, low, high], axis=1)


WIDE = 384
ROW_JK, ROW_IK, ROW_DIV, ROW_INT, ROW_LAY, ROW_BACK, ROW_END = 0, 192, 320, 384, 496, 608, 704


def constant_tables():
    diff = node_tables().astype(np.float32).astype(np.float64)
    sine, eigen = schwarz_tables()
    sine = sine.astype(np.float32).astype(np.float64)
    one = np.eye(NP)
    first, second = np.kron(diff, one), np.kron(one, diff)
    plane = np.concatenate([first, second, first @ first + second @ second], axis=0)
    along = np.concatenate([first, first @ first], axis=0)
    table = np.zeros((ROW_END, WIDE), jnp.bfloat16)
    table[ROW_JK : ROW_JK + 192, :192] = three(plane)
    table[ROW_IK : ROW_IK + 128, :192] = three(along)
    table[ROW_DIV : ROW_DIV + 64, :384] = np.concatenate([three(first), three(second)], axis=1)
    both = np.kron(sine, sine)
    grid = np.arange(100).reshape(10, 10)
    inner = grid[1:9, 1:9].reshape(-1)
    layers = np.concatenate([grid[0, 1:9], grid[9, 1:9], grid[1:9, 0], grid[1:9, 9]])
    forward = np.zeros((MODES16, 100))
    forward[:100] = both
    table[ROW_INT : ROW_INT + MODES16, :192] = three(forward[:, inner])
    table[ROW_LAY : ROW_LAY + MODES16, :96] = three(forward[:, layers])
    backward = np.zeros((96, MODES16))
    backward[:, :100] = both[np.concatenate([inner, layers])]
    table[ROW_BACK : ROW_BACK + 96, : 3 * MODES16] = three(backward)
    sums = np.zeros((MODES,))
    sums[:100] = (eigen[:, None] + eigen[None, :]).reshape(-1)
    sums = np.tile(sums[:, None], (1, 128)).astype(np.float32)
    return table, sums


def split(x):
    high = x.astype(BF16)
    low = (x - high.astype(F32)).astype(BF16)
    return high, low


def stack(x):
    high, low = split(x)
    return jnp.concatenate([high, high, low], axis=0)


def ld(ref, at, size):
    half = ref.shape[0] // 2
    return jnp.concatenate([ref[pl.ds(at, size), :], ref[pl.ds(half + at, size), :]], axis=1)


def st(ref, at, value):
    half, size = ref.shape[0] // 2, value.shape[0]
    ref[pl.ds(at, size), :] = value[:, :128]
    ref[pl.ds(half + at, size), :] = value[:, 128:]


def add(ref, at, value):
    st(ref, at, ld(ref, at, value.shape[0]) + value)


def ends_of(ref, at, k):
    half = ref.shape[0] // 2
    return [pl.ds(h * half + at + k, 64, stride=8) for h in range(2)]


def dot(a, b):
    return lax.dot_general(a, b, (((1,), (0,)), ((), ())), preferred_element_type=F32)


def dot_nt(a, b):
    return lax.dot_general(a, b, (((1,), (1,)), ((), ())), preferred_element_type=F32)


def kernel(
    leaves, lobes,
    base_hbm, adj_hbm, size_hbm, slot_hbm, table_hbm, sums_hbm,
    out_hbm, press_hbm,
    base, v0, v1, v2, grads, part, res, modes, recip, press, outer,
    size, slot, table, sums,
    zs, zr, zs1, zr1, msg, recv, a_lo, a_hi, chain_out, chain_in,
    in_sem, out_sem, z_send, z_recv, l_send, l_recv,
):
    me = lax.axis_index("leaf")
    lobe = lax.axis_index("lobe")
    rows = leaves * 8
    sine, eigen = schwarz_tables()

    loads = [
        pltpu.make_async_copy(slot_hbm, slot, in_sem.at[0]),
        pltpu.make_async_copy(adj_hbm.at[:, 0:128], v0.at[0:1536], in_sem.at[1]),
        pltpu.make_async_copy(table_hbm, table, in_sem.at[2]),
        pltpu.make_async_copy(size_hbm, size, in_sem.at[3]),
        pltpu.make_async_copy(base_hbm, base, in_sem.at[4]),
        pltpu.make_async_copy(sums_hbm, sums, in_sem.at[5]),
        pltpu.make_async_copy(adj_hbm.at[:, 128:256], v0.at[1536:3072], in_sem.at[6]),
    ]
    for load in loads:
        load.start()

    for x in range(4):
        recv[x, pl.ds(pl.multiple_of(me * 8, 8), 8), :] = jnp.zeros((8, 128), F32)

    @pl.when(lobe == 0)
    def _():
        zr[:, 0] = jnp.zeros((2, 192, EL), F32)
        zr1[:, 0] = jnp.zeros((2, 64, EL), F32)

    @pl.when(lobe == lobes - 1)
    def _():
        zr[:, 1] = jnp.zeros((2, 192, EL), F32)
        zr1[:, 1] = jnp.zeros((2, 64, EL), F32)

    barrier = pltpu.get_barrier_semaphore()

    def greet(d, carry):
        pl.semaphore_signal(
            barrier, inc=1, device_id={"leaf": lax.rem(me + d, leaves)},
            device_id_type=pl.DeviceIdType.MESH,
        )
        return carry

    lax.fori_loop(1, leaves, greet, 0)

    @pl.when(lobe > 0)
    def _():
        pl.semaphore_signal(
            barrier, inc=1, device_id={"lobe": lobe - 1}, device_id_type=pl.DeviceIdType.MESH
        )

    @pl.when(lobe < lobes - 1)
    def _():
        pl.semaphore_signal(
            barrier, inc=1, device_id={"lobe": lobe + 1}, device_id_type=pl.DeviceIdType.MESH
        )

    loads[0].wait()
    hot = (lax.broadcasted_iota(jnp.int32, (512, leaves * 4), 0) == slot[...]).astype(F32)
    row = lax.broadcasted_iota(jnp.int32, (rows, leaves * 4), 0)
    col = lax.broadcasted_iota(jnp.int32, (rows, leaves * 4), 1)
    spread = ((row >> 3) * 4 + (row & 3) == col).astype(F32)
    all_hot = dot_nt(spread.astype(BF16), hot.astype(BF16))
    low_row = (lax.broadcasted_iota(jnp.int32, (rows, 512), 0) & 4) == 0
    a_lo[...] = jnp.where(low_row, all_hot, 0.0).astype(BF16)
    a_hi[...] = jnp.where(low_row, 0.0, all_hot).astype(BF16)
    for cc in range(3):
        row = lax.broadcasted_iota(jnp.int32, (rows, 128), 0)
        col = lax.broadcasted_iota(jnp.int32, (rows, 128), 1)
        after, before = (me + 1) * 8 + 4 + cc, (me - 1) * 8 + 4 + cc
        pick = ((row == after) & (col == 127)) | ((row == before) & (col == 0))
        chain_out[:, cc * 128 : cc * 128 + 128] = pick.astype(F32).astype(BF16)
        row = lax.broadcasted_iota(jnp.int32, (rows, EL), 0)
        col = lax.broadcasted_iota(jnp.int32, (rows, EL), 1)
        put = ((row == before) & (col == 0)) | ((row == after) & (col == EL - 1))
        chain_in[:, cc * EL : (cc + 1) * EL] = put.astype(F32).astype(BF16)

    def start_z(sends, recvs, at, x):
        @pl.when(lobe < lobes - 1)
        def _():
            pltpu.make_async_remote_copy(
                sends.at[at, 1], recvs.at[at, 0], z_send.at[x, 1], z_recv.at[x, 0],
                device_id={"lobe": lobe + 1}, device_id_type=pl.DeviceIdType.MESH,
            ).start()

        @pl.when(lobe > 0)
        def _():
            pltpu.make_async_remote_copy(
                sends.at[at, 0], recvs.at[at, 1], z_send.at[x, 0], z_recv.at[x, 1],
                device_id={"lobe": lobe - 1}, device_id_type=pl.DeviceIdType.MESH,
            ).start()

    def wait_z(sends, recvs, at, x, sent):
        @pl.when(lobe < lobes - 1)
        def _():
            copy = pltpu.make_async_remote_copy(
                sends.at[at, 1], recvs.at[at, 1], z_send.at[x, 1], z_recv.at[x, 1],
                device_id={"lobe": lobe + 1}, device_id_type=pl.DeviceIdType.MESH,
            )
            copy.wait_send() if sent else copy.wait_recv()

        @pl.when(lobe > 0)
        def _():
            copy = pltpu.make_async_remote_copy(
                sends.at[at, 0], recvs.at[at, 0], z_send.at[x, 0], z_recv.at[x, 0],
                device_id={"lobe": lobe - 1}, device_id_type=pl.DeviceIdType.MESH,
            )
            copy.wait_send() if sent else copy.wait_recv()

    def start_links(x):
        def body(d, carry):
            peer = lax.rem(me + d, leaves)
            pltpu.make_async_remote_copy(
                msg.at[x, pl.ds(pl.multiple_of(peer * 8, 8), 8)],
                recv.at[x, pl.ds(pl.multiple_of(me * 8, 8), 8)],
                l_send.at[x], l_recv.at[x],
                device_id={"leaf": peer}, device_id_type=pl.DeviceIdType.MESH,
            ).start()
            return carry

        lax.fori_loop(1, leaves, body, 0)

    def wait_links(x, sent):
        copy = pltpu.make_async_remote_copy(
            msg.at[x, pl.ds(0, rows - 8)], recv.at[x, pl.ds(0, rows - 8)],
            l_send.at[x], l_recv.at[x],
            device_id={"leaf": lax.rem(me + 1, leaves)}, device_id_type=pl.DeviceIdType.MESH,
        )
        copy.wait_send() if sent else copy.wait_recv()

    def zeros64(width):
        return jnp.zeros((64, width), F32)

    def fill_message(x, face2, face3, leads, tails):
        count = len(leads)
        total = jnp.zeros((rows, 128), F32)
        lane = lax.broadcasted_iota(jnp.int32, (64, 128), 1)
        for f, face in enumerate((face2, face3)):
            if count == 3:
                for piece in split(face[:128]):
                    total += dot_nt(a_lo[:, f * EL : (f + 1) * EL], piece)
            last = jnp.concatenate([face[-64:], zeros64(EL)], axis=0)
            for piece in split(last):
                total += dot_nt(a_hi[:, f * EL : (f + 1) * EL], piece)
        for cc in range(count):
            ends = jnp.where(lane == 0, leads[cc], jnp.where(lane == 127, tails[cc], 0.0))
            ends = jnp.concatenate([zeros64(128), ends], axis=0)
            for piece in split(ends):
                total += dot_nt(chain_out[:, cc * 128 : (cc + 1) * 128], piece)
        msg[x] = total

    def read_links(x, count):
        turned = jnp.transpose(recv[x])
        high, low = split(turned)
        near = []
        if count == 3:
            near.append(dot(high, a_lo[...]) + dot(low, a_lo[...]))
        near.append((dot(high, a_hi[...]) + dot(low, a_hi[...]))[:64])
        near = jnp.concatenate(near, axis=0) if count == 3 else near[0]
        wide = count * EL
        ends = dot(high[64:], chain_in[:, :wide]) + dot(low[64:], chain_in[:, :wide])
        return near, ends

    def spot(c, i):
        return pl.multiple_of(c * 512 + i * 64, 64)

    def block(c, i):
        return pl.ds(spot(c, i), 64)

    def across(ref, c, j):
        at = [pl.multiple_of(c * 512 + i * 64 + j * 8, 8) for i in range(8)]
        if ref.shape[1] == 128:
            return jnp.concatenate([ld(ref, one, 8) for one in at], axis=0)
        return jnp.concatenate([ref[pl.ds(one, 8), :] for one in at], axis=0)

    def put_across(ref, c, j, value):
        for i in range(8):
            at = pl.multiple_of(c * 512 + i * 64 + j * 8, 8)
            if ref.shape[1] == 128:
                st(ref, at, value[i * 8 : i * 8 + 8])
            else:
                ref[pl.ds(at, 8), :] = value[i * 8 : i * 8 + 8]

    lane = lax.broadcasted_iota(jnp.int32, (64, EL), 1)

    def chain_near(lead, tail):
        near0 = jnp.where(lane == 0, 0.0, pltpu.roll(tail, 1, 1))
        near1 = jnp.where(lane == EL - 1, 0.0, pltpu.roll(lead, EL - 1, 1))
        return near0, near1

    def send_faces(v, x):
        for c in range(3):
            for side, k in ((0, 0), (1, 7)):
                for h, at in enumerate(ends_of(v, c * 512, k)):
                    zs[x, side, c * 64 : c * 64 + 64, h * 128 : h * 128 + 128] = v[at, :]
        if x == 0:
            pl.semaphore_wait(
                barrier,
                leaves - 1 + (lobe > 0).astype(jnp.int32) + (lobe < lobes - 1).astype(jnp.int32),
            )
        start_z(zs, zr, x, x)
        face2 = jnp.concatenate(
            [ld(v, c * 512 + i * 64, 8) for c in range(3) for i in range(8)], axis=0
        )
        face3 = jnp.concatenate(
            [ld(v, c * 512 + i * 64 + 56, 8) for c in range(3) for i in range(8)], axis=0
        )
        leads = [v[c * 512 : c * 512 + 64, :] for c in range(3)]
        tails = [v[1536 + c * 512 + 448 : 1536 + c * 512 + 512, :] for c in range(3)]
        fill_message(x, face2, face3, leads, tails)
        start_links(x)

    def advance(v, w, x):
        scale = 2.0 / size[...]
        visc = viscosity * scale
        step = time_step * scale

        def one(j, carry):
            for c in range(3):
                y = dot(table[ROW_IK : ROW_IK + 128, :192], stack(across(v, c, j)))
                put_across(part, c, j, across(base, 0, j) * y[:64] + visc * y[64:])
            return carry

        lax.fori_loop(0, 8, one, 0, unroll=2)
        sub = lax.broadcasted_iota(jnp.int32, (64, EL), 0)
        k, j = sub & 7, sub >> 3
        edge = ((k == 0) | (k == 7)).astype(F32) + ((j == 0) | (j == 7)).astype(F32)

        def two(i, carry):
            own = [ld(v, spot(r, i), 64) for r in range(3)]
            b1, b2 = base[block(1, i), :], base[block(2, i), :]
            ends = jnp.where((i == 0) | (i == 7), 1.0, 0.0).astype(F32)
            keep = 1.0 - penalty * (edge + ends)
            for c in range(3):
                y = dot(table[ROW_JK : ROW_JK + 192, :192], stack(own[c]))
                total = part[block(c, i), :] + b1 * y[:64] + b2 * y[64:128] + visc * y[128:]
                for r in range(3):
                    total -= own[r] * grads[block(c * 3 + r, i), :]
                st(w, spot(c, i), keep * own[c] + step * total)
            return carry

        lax.fori_loop(0, 8, two, 0, unroll=2)
        for c in range(3):
            near0, near1 = chain_near(ld(v, spot(c, 0), 64), ld(v, spot(c, 7), 64))
            add(w, spot(c, 0), penalty * near0)
            add(w, spot(c, 7), penalty * near1)
        wait_links(x, False)
        near, ends = read_links(x, 3)
        for c in range(3):
            end = ends[:, c * EL : (c + 1) * EL]
            add(w, spot(c, 0), jnp.where(lane == 0, penalty * end, 0.0))
            add(w, spot(c, 7), jnp.where(lane == EL - 1, penalty * end, 0.0))
            for i in range(8):
                for f, j in ((0, 0), (1, 7)):
                    at = c * 512 + i * 64 + j * 8
                    r0 = c * 64 + i * 8
                    add(w, at, penalty * near[r0 : r0 + 8, f * EL : (f + 1) * EL])
        wait_z(zs, zr, x, x, False)
        for c in range(3):
            for side, k in ((0, 0), (1, 7)):
                for h, at in enumerate(ends_of(w, c * 512, k)):
                    near = zr[x, side, c * 64 : c * 64 + 64, h * 128 : h * 128 + 128]
                    w[at, :] = w[at, :] + penalty * near

    loads[1].wait()
    loads[6].wait()
    send_faces(v0, 0)
    loads[2].wait()
    loads[3].wait()
    loads[4].wait()
    loads[5].wait()

    def grad_one(j, carry):
        for r in range(3):
            y = dot(table[ROW_IK : ROW_IK + 64, :192], stack(across(base, r, j)))
            put_across(grads, r, j, y)
        return carry

    lax.fori_loop(0, 8, grad_one, 0, unroll=2)

    def grad_two(i, carry):
        for r in range(3):
            y = dot(table[ROW_JK : ROW_JK + 128, :192], stack(base[block(r, i), :]))
            grads[block(3 + r, i), :] = y[:64]
            grads[block(6 + r, i), :] = y[64:]
        return carry

    lax.fori_loop(0, 8, grad_two, 0, unroll=2)
    advance(v0, v1, 0)

    send_faces(v1, 1)
    scale_square = (1.0 / size[...]) ** 2

    def recip_body(b, carry):
        at = pl.multiple_of(b * 8, 8)
        here = sums[pl.ds(at, 8), :]
        here = jnp.concatenate([here, here], axis=1)
        for m in range(10):
            recip[pl.ds(pl.multiple_of(m * MODES + at, 8), 8), :] = 1.0 / (
                (here + float(eigen[m])) * scale_square + shift_term
            )
        return carry

    lax.fori_loop(0, MODES // 8, recip_body, 0)
    advance(v1, v2, 1)
    out_copies = [
        pltpu.make_async_copy(v2.at[h * 1536 : h * 1536 + 1536], out_hbm.at[:, h * 128 : h * 128 + 128], out_sem.at[h])
        for h in range(2)
    ]
    for copy in out_copies:
        copy.start()

    scale = 2.0 / size[...]

    def div_one(j, carry):
        put_across(res, 0, j, dot(table[ROW_IK : ROW_IK + 64, :192], stack(across(v2, 0, j))))
        return carry

    lax.fori_loop(0, 8, div_one, 0, unroll=4)

    def div_two(i, carry):
        both = jnp.concatenate([stack(ld(v2, spot(1, i), 64)), stack(ld(v2, spot(2, i), 64))], axis=0)
        y = dot(table[ROW_DIV : ROW_DIV + 64, :], both)
        st(res, spot(0, i), scale * (ld(res, spot(0, i), 64) + y))
        return carry

    lax.fori_loop(0, 8, div_two, 0, unroll=4)
    for side, k in ((0, 0), (1, 7)):
        for h, at in enumerate(ends_of(res, 0, k)):
            zs1[0, side, :, h * 128 : h * 128 + 128] = res[at, :]
    start_z(zs1, zr1, 0, 2)
    face2 = jnp.concatenate([ld(res, i * 64, 8) for i in range(8)], axis=0)
    face3 = jnp.concatenate([ld(res, i * 64 + 56, 8) for i in range(8)], axis=0)
    fill_message(2, face2, face3, [res[0:64, :]], [res[512 + 448 : 512 + 512, :]])
    start_links(2)

    def forward(i, carry):
        y = dot(table[ROW_INT : ROW_INT + MODES16, :192], stack(ld(res, spot(0, i), 64)))
        modes[pl.ds(pl.multiple_of((i + 1) * MODES, 8), MODES), :] = y[:MODES]
        return carry

    lax.fori_loop(0, 8, forward, 0, unroll=4)
    near0, near1 = chain_near(ld(res, 0, 64), ld(res, 448, 64))
    wait_links(2, False)
    near, ends = read_links(2, 1)
    near0 = jnp.where(lane == 0, ends, near0)
    near1 = jnp.where(lane == EL - 1, ends, near1)
    for n, plane in ((0, near0), (9, near1)):
        y = dot(table[ROW_INT : ROW_INT + MODES16, :192], stack(plane))
        modes[n * MODES : (n + 1) * MODES, :] = y[:MODES]
    wait_z(zs1, zr1, 0, 2, False)
    for i in range(8):
        r0 = slice(i * 8, i * 8 + 8)
        layer = jnp.concatenate(
            [near[r0, :EL], near[r0, EL:], zr1[0, 0, r0, :], zr1[0, 1, r0, :]], axis=0
        )
        y = dot(table[ROW_LAY : ROW_LAY + MODES16, :96], stack(layer))
        modes[(i + 1) * MODES : (i + 2) * MODES, :] += y[:MODES]

    def along(values):
        plus = [values[n] + values[9 - n] for n in range(5)]
        minus = [values[n] - values[9 - n] for n in range(5)]
        result = []
        for m in range(10):
            terms = plus if m % 2 == 0 else minus
            total = terms[0] * float(np.float32(sine[m, 0]))
            for n in range(1, 5):
                total += terms[n] * float(np.float32(sine[m, n]))
            result.append(total)
        return result

    def solve(b, carry):
        at = [pl.ds(pl.multiple_of(m * MODES + b * 8, 8), 8) for m in range(10)]
        values = along([modes[at[m], :] for m in range(10)])
        values = along([values[m] * recip[at[m], :] for m in range(10)])
        for m in range(10):
            modes[at[m], :] = values[m]
        return carry

    lax.fori_loop(0, MODES // 8, solve, 0)

    pad = jnp.zeros((MODES16 - MODES, EL), F32)
    for n, at in ((0, 0), (9, 64)):
        plane = jnp.concatenate([modes[n * MODES : (n + 1) * MODES, :], pad], axis=0)
        outer[at : at + 64, :] = dot(table[ROW_BACK : ROW_BACK + 64, : 3 * MODES16], stack(plane))

    def backward(i, carry):
        plane = modes[pl.ds(pl.multiple_of((i + 1) * MODES, 8), MODES), :]
        plane = jnp.concatenate([plane, pad], axis=0)
        y = dot(table[ROW_BACK : ROW_BACK + 96, : 3 * MODES16], stack(plane))
        st(press, spot(0, i), y[:64])
        r0 = pl.multiple_of(i * 8, 8)
        outer[pl.ds(128 + r0, 8), :] = y[64:72]
        outer[pl.ds(192 + r0, 8), :] = y[72:80]
        zs1[1, 0, pl.ds(r0, 8), :] = y[80:88]
        zs1[1, 1, pl.ds(r0, 8), :] = y[88:96]
        return carry

    lax.fori_loop(0, 8, backward, 0, unroll=4)
    start_z(zs1, zr1, 1, 3)
    fill_message(
        3, outer[128:192, :], outer[192:256, :], [outer[0:64, 0:128]], [outer[64:128, 128:256]]
    )
    start_links(3)
    near0, near1 = chain_near(outer[0:64, :], outer[64:128, :])
    wait_links(3, False)
    near, ends = read_links(3, 1)
    add(press, 0, jnp.where(lane == 0, ends, near0))
    add(press, 448, jnp.where(lane == EL - 1, ends, near1))
    for i in range(8):
        for f, j in ((0, 0), (1, 7)):
            at = i * 64 + j * 8
            add(press, at, near[i * 8 : i * 8 + 8, f * EL : (f + 1) * EL])
    wait_z(zs1, zr1, 1, 3, False)
    for side, k in ((0, 0), (1, 7)):
        for h, at in enumerate(ends_of(press, 0, k)):
            press[at, :] = press[at, :] + zr1[1, side, :, h * 128 : h * 128 + 128]
    press_copies = [
        pltpu.make_async_copy(press.at[h * 512 : h * 512 + 512], press_hbm.at[:, h * 128 : h * 128 + 128], out_sem.at[2 + h])
        for h in range(2)
    ]
    for copy in press_copies:
        copy.start()
    for x in range(4):
        wait_links(x, True)
        if x < 2:
            wait_z(zs, zr, x, x, True)
        else:
            wait_z(zs1, zr1, x - 2, x, True)
    for copy in out_copies + press_copies:
        copy.wait()


def local(leaves, lobes, base_velocity, adjoint_velocity, element_size, link_slot):
    table, sums = constant_tables()
    rows = leaves * 8
    any_space = pl.BlockSpec(memory_space=pl.ANY)
    scratch = [
        pltpu.VMEM((1536, EL), F32),
        pltpu.VMEM((3072, 128), F32),
        pltpu.VMEM((3072, 128), F32),
        pltpu.VMEM((3072, 128), F32),
        pltpu.VMEM((9 * 512, EL), F32),
        pltpu.VMEM((1536, EL), F32),
        pltpu.VMEM((1024, 128), F32),
        pltpu.VMEM((10 * MODES, EL), F32),
        pltpu.VMEM((10 * MODES, EL), F32),
        pltpu.VMEM((1024, 128), F32),
        pltpu.VMEM((256, EL), F32),
        pltpu.VMEM((1, EL), F32),
        pltpu.VMEM((1, leaves * 4), jnp.int32),
        pltpu.VMEM((ROW_END, WIDE), BF16),
        pltpu.VMEM((MODES, 128), F32),
        pltpu.VMEM((2, 2, 192, EL), F32),
        pltpu.VMEM((2, 2, 192, EL), F32),
        pltpu.VMEM((2, 2, 64, EL), F32),
        pltpu.VMEM((2, 2, 64, EL), F32),
        pltpu.VMEM((4, rows, 128), F32),
        pltpu.VMEM((4, rows, 128), F32),
        pltpu.VMEM((rows, 512), BF16),
        pltpu.VMEM((rows, 512), BF16),
        pltpu.VMEM((rows, 384), BF16),
        pltpu.VMEM((rows, 768), BF16),
        pltpu.SemaphoreType.DMA((7,)),
        pltpu.SemaphoreType.DMA((4,)),
        pltpu.SemaphoreType.DMA((4, 2)),
        pltpu.SemaphoreType.DMA((4, 2)),
        pltpu.SemaphoreType.DMA((4,)),
        pltpu.SemaphoreType.DMA((4,)),
    ]
    out, press = pl.pallas_call(
        functools.partial(kernel, leaves, lobes),
        out_shape=(
            jax.ShapeDtypeStruct((1536, EL), F32),
            jax.ShapeDtypeStruct((512, EL), F32),
        ),
        in_specs=[any_space] * 6,
        out_specs=(any_space, any_space),
        scratch_shapes=scratch,
        compiler_params=pltpu.CompilerParams(
            collective_id=0, has_side_effects=True, vmem_limit_bytes=40 * 1024 * 1024
        ),
    )(
        base_velocity.reshape(1536, EL),
        adjoint_velocity.reshape(1536, EL),
        element_size.reshape(1, EL),
        link_slot.reshape(1, leaves * 4),
        jnp.asarray(table),
        jnp.asarray(sums),
    )
    return out.reshape(3, 512, EL), press


def solution(mesh):
    placed = (
        P(None, None, ("leaf", "lobe")),
        P(None, None, ("leaf", "lobe")),
        P(("leaf", "lobe")),
        P(("leaf", "lobe")),
    )
    return jax.shard_map(
        functools.partial(local, mesh.shape["leaf"], mesh.shape["lobe"]),
        mesh=mesh,
        in_specs=placed,
        out_specs=(P(None, None, ("leaf", "lobe")), P(None, ("leaf", "lobe"))),
        check_vma=False,
    )
```

profile of v0, /device:TPU:97, one launch (start us, length us, event | category | flops | bytes accessed | tf_op | source)
XLA Modules:
  0.0 45.2 jit_solution(14122833833482269455)
XLA Ops:
  0.6 0.0 copy-start
  0.6 1.4 %copy-done = f32[3,512,256]{2,1,0:T(8,128)S(1)} copy-done((f32[3,512,256]{2,1,0:T(8,128)S(1)}, f32[3,512,256]{2,1,0:T(8,128)}, u32[]{:S(2)}) %copy-start) | copy-done | bytes 1572888
  2.0 0.0 copy-start.1
  2.0 1.4 %copy-done.1 = f32[3,512,256]{2,1,0:T(8,128)S(1)} copy-done((f32[3,512,256]{2,1,0:T(8,128)S(1)}, f32[3,512,256]{2,1,0:T(8,128)}, u32[]{:S(2)}) %copy-start.1) | copy-done | bytes 1572888
  3.4 0.0 copy-start.2
  3.5 1.0 %copy-done.2 = bf16[704,384]{1,0:T(8,128)(2,1)S(1)} copy-done((bf16[704,384]{1,0:T(8,128)(2,1)S(1)}, bf16[704,384]{1,0:T(8,128)(2,1)}, u32[]{:S(2)}) %copy-start.2) | copy-done | bytes 540696
  4.5 0.0 copy-start.3
  4.5 0.8 %copy-done.3 = f32[104,128]{1,0:T(8,128)S(1)} copy-done((f32[104,128]{1,0:T(8,128)S(1)}, f32[104,128]{1,0:T(8,128)}, u32[]{:S(2)}) %copy-start.3) | copy-done | bytes 53272
  5.3 0.0 copy-start.4
  5.3 0.7 %copy-done.4 = f32[256]{0:T(256)S(1)} copy-done((f32[256]{0:T(256)S(1)}, f32[256]{0:T(256)}, u32[]{:S(2)}) %copy-start.4) | copy-done | bytes 1048
  6.0 0.0 copy-start.5
  6.0 0.7 %copy-done.5 = s32[128]{0:T(128)S(1)} copy-done((s32[128]{0:T(128)S(1)}, s32[128]{0:T(128)}, u32[]{:S(2)}) %copy-start.5) | copy-done | bytes 536
  6.6 36.6 %shard_map.77 = (f32[1536,256]{1,0:T(8,128)S(1)}, f32[512,256]{1,0:T(8,128)S(1)}) custom-call(f32[1536,256]{1,0:T(8,128)S(1)} %bitcast.6, f32[1536,256]{1,0:T(8,128)S(1)} %bitcast.7, f32[1,256]{1,0:T(1,128)S(1)} %bitcast.8, s32[1,128]{1,0:T(1,128)S(1)} %bitcast.9, bf16[704,384]{1,0:T(8,128)(2,1)S(1)} %copy-done.2, f32[104,128]{1,0:T(8,128)S(1)} %copy-done.3), custom_call_target="tpu_custom_call" | custom-call | tf_op jit(solution)/shard_map/pallas_call | solution.py:622
  43.3 1.1 %copy.10 = f32[3,512,256]{2,1,0:T(8,128)} copy(f32[3,512,256]{2,1,0:T(8,128)S(1)} %bitcast.5) | data formatting | bytes 3145728
  44.4 0.8 %copy.11 = f32[512,256]{1,0:T(8,128)} copy(f32[512,256]{1,0:T(8,128)S(1)} %get-tuple-element.9) | data formatting | bytes 1048576
Async XLA Ops:
  0.6 1.4 %copy-start = (f32[3,512,256]{2,1,0:T(8,128)S(1)}, f32[3,512,256]{2,1,0:T(8,128)}, u32[]{:S(2)}) copy-start(f32[3,512,256]{2,1,0:T(8,128)} %param.6) | copy-start | bytes 4718596
  2.0 1.4 %copy-start.1 = (f32[3,512,256]{2,1,0:T(8,128)S(1)}, f32[3,512,256]{2,1,0:T(8,128)}, u32[]{:S(2)}) copy-start(f32[3,512,256]{2,1,0:T(8,128)} %param.7) | copy-start | bytes 4718596
  3.4 1.0 %copy-start.2 = (bf16[704,384]{1,0:T(8,128)(2,1)S(1)}, bf16[704,384]{1,0:T(8,128)(2,1)}, u32[]{:S(2)}) copy-start(bf16[704,384]{1,0:T(8,128)(2,1)} %constant.4.clone.table_hbm) | copy-start | bytes 1622020
  4.5 0.8 %copy-start.3 = (f32[104,128]{1,0:T(8,128)S(1)}, f32[104,128]{1,0:T(8,128)}, u32[]{:S(2)}) copy-start(f32[104,128]{1,0:T(8,128)} %constant.5.clone.sums_hbm) | copy-start | bytes 159748
  5.3 0.7 %copy-start.4 = (f32[256]{0:T(256)S(1)}, f32[256]{0:T(256)}, u32[]{:S(2)}) copy-start(f32[256]{0:T(256)} %param.8) | copy-start | bytes 3076
  6.0 0.7 %copy-start.5 = (s32[128]{0:T(128)S(1)}, s32[128]{0:T(128)}, u32[]{:S(2)}) copy-start(s32[128]{0:T(128)} %param.9) | copy-start | bytes 1540
where the time goes:
time: 45.7 us; the launch traced here: 45.2 us
  Pallas kernels  36.6 us (80%)
  local copies, waits for them, and re-layouts  7.93 us (17%)
  between operations  0.65 us (1%)
    pallas_call x1, Pallas kernels, local(): pl.pallas_call(functools.partial(kernel, leaves, lobes), out_shape=(jax.S...  36.6 us
    unnamed x14, local copies, waits for them, and re-layouts  7.93 us

commit v1 on v0

--- a/solution.py
+++ b/solution.py
@@ -10,6 +10,7 @@
 from jax.sharding import PartitionSpec as P
 
 NP = 8
+PIECES = 3
 EL = 256
 MODES = 104
 MODES16 = 112
@@ -144,6 +145,19 @@
     return lax.dot_general(a, b, (((1,), (1,)), ((), ())), preferred_element_type=F32)
 
 
+def far_first(me, leaves):
+    if leaves != 32:
+        return [lax.rem(me + d, leaves) for d in range(1, leaves)]
+    hops = [0, 1, 2, 1]
+    steps = [(dy, dx, dc) for dy in range(4) for dx in range(4) for dc in range(2)][1:]
+    steps.sort(key=lambda one: -(hops[one[0]] + hops[one[1]]))
+    y, x, core = me // 8, lax.rem(me // 2, 4), lax.rem(me, 2)
+    return [
+        lax.rem(y + dy, 4) * 8 + lax.rem(x + dx, 4) * 2 + lax.rem(core + dc, 2)
+        for dy, dx, dc in steps
+    ]
+
+
 def kernel(
     leaves, lobes,
     base_hbm, adj_hbm, size_hbm, slot_hbm, table_hbm, sums_hbm,
@@ -158,6 +172,25 @@
     rows = leaves * 8
     sine, eigen = schwarz_tables()
 
+    barrier = pltpu.get_barrier_semaphore()
+    peers = far_first(me, leaves)
+    for peer in peers:
+        pl.semaphore_signal(
+            barrier, inc=1, device_id={"leaf": peer}, device_id_type=pl.DeviceIdType.MESH
+        )
+
+    @pl.when(lobe > 0)
+    def _():
+        pl.semaphore_signal(
+            barrier, inc=1, device_id={"lobe": lobe - 1}, device_id_type=pl.DeviceIdType.MESH
+        )
+
+    @pl.when(lobe < lobes - 1)
+    def _():
+        pl.semaphore_signal(
+            barrier, inc=1, device_id={"lobe": lobe + 1}, device_id_type=pl.DeviceIdType.MESH
+        )
+
     loads = [
         pltpu.make_async_copy(slot_hbm, slot, in_sem.at[0]),
         pltpu.make_async_copy(adj_hbm.at[:, 0:128], v0.at[0:1536], in_sem.at[1]),
@@ -182,29 +215,6 @@
     def _():
         zr[:, 1] = jnp.zeros((2, 192, EL), F32)
         zr1[:, 1] = jnp.zeros((2, 64, EL), F32)
-
-    barrier = pltpu.get_barrier_semaphore()
-
-    def greet(d, carry):
-        pl.semaphore_signal(
-            barrier, inc=1, device_id={"leaf": lax.rem(me + d, leaves)},
-            device_id_type=pl.DeviceIdType.MESH,
-        )
-        return carry
-
-    lax.fori_loop(1, leaves, greet, 0)
-
-    @pl.when(lobe > 0)
-    def _():
-        pl.semaphore_signal(
-            barrier, inc=1, device_id={"lobe": lobe - 1}, device_id_type=pl.DeviceIdType.MESH
-        )
-
-    @pl.when(lobe < lobes - 1)
-    def _():
-        pl.semaphore_signal(
-            barrier, inc=1, device_id={"lobe": lobe + 1}, device_id_type=pl.DeviceIdType.MESH
-        )
 
     loads[0].wait()
     hot = (lax.broadcasted_iota(jnp.int32, (512, leaves * 4), 0) == slot[...]).astype(F32)
@@ -226,50 +236,50 @@
         put = ((row == before) & (col == 0)) | ((row == after) & (col == EL - 1))
         chain_in[:, cc * EL : (cc + 1) * EL] = put.astype(F32).astype(BF16)
 
-    def start_z(sends, recvs, at, x):
+    def z_copies(sends, recvs, at, x, c):
+        rows_of = pl.ds(c * 64, 64)
+        up = pltpu.make_async_remote_copy(
+            sends.at[at, 1, rows_of], recvs.at[at, 0, rows_of],
+            z_send.at[x, 1, c], z_recv.at[x, 0, c],
+            device_id={"lobe": lobe + 1}, device_id_type=pl.DeviceIdType.MESH,
+        )
+        down = pltpu.make_async_remote_copy(
+            sends.at[at, 0, rows_of], recvs.at[at, 1, rows_of],
+            z_send.at[x, 0, c], z_recv.at[x, 1, c],
+            device_id={"lobe": lobe - 1}, device_id_type=pl.DeviceIdType.MESH,
+        )
+        return up, down
+
+    def start_z(sends, recvs, at, x, c):
+        up, down = z_copies(sends, recvs, at, x, c)
+
         @pl.when(lobe < lobes - 1)
         def _():
-            pltpu.make_async_remote_copy(
-                sends.at[at, 1], recvs.at[at, 0], z_send.at[x, 1], z_recv.at[x, 0],
-                device_id={"lobe": lobe + 1}, device_id_type=pl.DeviceIdType.MESH,
-            ).start()
+            up.start()
 
         @pl.when(lobe > 0)
         def _():
-            pltpu.make_async_remote_copy(
-                sends.at[at, 0], recvs.at[at, 1], z_send.at[x, 0], z_recv.at[x, 1],
-                device_id={"lobe": lobe - 1}, device_id_type=pl.DeviceIdType.MESH,
-            ).start()
-
-    def wait_z(sends, recvs, at, x, sent):
+            down.start()
+
+    def wait_z(sends, recvs, at, x, c, sent):
+        up, down = z_copies(sends, recvs, at, x, c)
+
         @pl.when(lobe < lobes - 1)
         def _():
-            copy = pltpu.make_async_remote_copy(
-                sends.at[at, 1], recvs.at[at, 1], z_send.at[x, 1], z_recv.at[x, 1],
-                device_id={"lobe": lobe + 1}, device_id_type=pl.DeviceIdType.MESH,
-            )
-            copy.wait_send() if sent else copy.wait_recv()
+            up.wait_send() if sent else down.wait_recv()
 
         @pl.when(lobe > 0)
         def _():
-            copy = pltpu.make_async_remote_copy(
-                sends.at[at, 0], recvs.at[at, 0], z_send.at[x, 0], z_recv.at[x, 0],
-                device_id={"lobe": lobe - 1}, device_id_type=pl.DeviceIdType.MESH,
-            )
-            copy.wait_send() if sent else copy.wait_recv()
+            down.wait_send() if sent else up.wait_recv()
 
     def start_links(x):
-        def body(d, carry):
-            peer = lax.rem(me + d, leaves)
+        for peer in peers:
             pltpu.make_async_remote_copy(
                 msg.at[x, pl.ds(pl.multiple_of(peer * 8, 8), 8)],
                 recv.at[x, pl.ds(pl.multiple_of(me * 8, 8), 8)],
                 l_send.at[x], l_recv.at[x],
                 device_id={"leaf": peer}, device_id_type=pl.DeviceIdType.MESH,
             ).start()
-            return carry
-
-        lax.fori_loop(1, leaves, body, 0)
 
     def wait_links(x, sent):
         copy = pltpu.make_async_remote_copy(
@@ -282,19 +292,22 @@
     def zeros64(width):
         return jnp.zeros((64, width), F32)
 
-    def fill_message(x, face2, face3, leads, tails):
-        count = len(leads)
+    def low_message(face2, face3):
         total = jnp.zeros((rows, 128), F32)
-        lane = lax.broadcasted_iota(jnp.int32, (64, 128), 1)
         for f, face in enumerate((face2, face3)):
-            if count == 3:
-                for piece in split(face[:128]):
-                    total += dot_nt(a_lo[:, f * EL : (f + 1) * EL], piece)
-            last = jnp.concatenate([face[-64:], zeros64(EL)], axis=0)
-            for piece in split(last):
+            for piece in split(face):
+                total += dot_nt(a_lo[:, f * EL : (f + 1) * EL], piece)
+        return total
+
+    def fill_message(x, total, face2, face3, leads, tails):
+        end_lane = lax.broadcasted_iota(jnp.int32, (64, 128), 1)
+        for f, face in enumerate((face2, face3)):
+            for piece in split(jnp.concatenate([face, zeros64(EL)], axis=0)):
                 total += dot_nt(a_hi[:, f * EL : (f + 1) * EL], piece)
-        for cc in range(count):
-            ends = jnp.where(lane == 0, leads[cc], jnp.where(lane == 127, tails[cc], 0.0))
+        for cc in range(len(leads)):
+            ends = jnp.where(
+                end_lane == 0, leads[cc], jnp.where(end_lane == 127, tails[cc], 0.0)
+            )
             ends = jnp.concatenate([zeros64(128), ends], axis=0)
             for piece in split(ends):
                 total += dot_nt(chain_out[:, cc * 128 : (cc + 1) * 128], piece)
@@ -339,26 +352,18 @@
         near1 = jnp.where(lane == EL - 1, 0.0, pltpu.roll(lead, EL - 1, 1))
         return near0, near1
 
-    def send_faces(v, x):
-        for c in range(3):
-            for side, k in ((0, 0), (1, 7)):
-                for h, at in enumerate(ends_of(v, c * 512, k)):
-                    zs[x, side, c * 64 : c * 64 + 64, h * 128 : h * 128 + 128] = v[at, :]
-        if x == 0:
-            pl.semaphore_wait(
-                barrier,
-                leaves - 1 + (lobe > 0).astype(jnp.int32) + (lobe < lobes - 1).astype(jnp.int32),
-            )
-        start_z(zs, zr, x, x)
-        face2 = jnp.concatenate(
-            [ld(v, c * 512 + i * 64, 8) for c in range(3) for i in range(8)], axis=0
-        )
-        face3 = jnp.concatenate(
-            [ld(v, c * 512 + i * 64 + 56, 8) for c in range(3) for i in range(8)], axis=0
-        )
+    def side(v, parts, j):
+        return jnp.concatenate(
+            [ld(v, c * 512 + i * 64 + j * 8, 8) for c in parts for i in range(8)], axis=0
+        )
+
+    def low_faces(v):
+        return low_message(side(v, (0, 1), 0), side(v, (0, 1), 7))
+
+    def send_links(v, x, total):
         leads = [v[c * 512 : c * 512 + 64, :] for c in range(3)]
         tails = [v[1536 + c * 512 + 448 : 1536 + c * 512 + 512, :] for c in range(3)]
-        fill_message(x, face2, face3, leads, tails)
+        fill_message(x, total, side(v, (2,), 0), side(v, (2,), 7), leads, tails)
         start_links(x)
 
     def advance(v, w, x):
@@ -406,16 +411,36 @@
                     at = c * 512 + i * 64 + j * 8
                     r0 = c * 64 + i * 8
                     add(w, at, penalty * near[r0 : r0 + 8, f * EL : (f + 1) * EL])
-        wait_z(zs, zr, x, x, False)
+        total = None
         for c in range(3):
-            for side, k in ((0, 0), (1, 7)):
+            wait_z(zs, zr, x, x, c, False)
+            for f, k in ((0, 0), (1, 7)):
                 for h, at in enumerate(ends_of(w, c * 512, k)):
-                    near = zr[x, side, c * 64 : c * 64 + 64, h * 128 : h * 128 + 128]
-                    w[at, :] = w[at, :] + penalty * near
+                    here = slice(c * 64, c * 64 + 64), slice(h * 128, h * 128 + 128)
+                    value = w[at, :] + penalty * zr[x, f, here[0], here[1]]
+                    w[at, :] = value
+                    if x == 0:
+                        zs[1, f, here[0], here[1]] = value
+            if x == 0:
+                start_z(zs, zr, 1, 1, c)
+                if c == 1:
+                    total = low_faces(w)
+        if x == 0:
+            send_links(w, 1, total)
 
     loads[1].wait()
     loads[6].wait()
-    send_faces(v0, 0)
+    for c in range(3):
+        for f, k in ((0, 0), (1, 7)):
+            for h, at in enumerate(ends_of(v0, c * 512, k)):
+                zs[0, f, c * 64 : c * 64 + 64, h * 128 : h * 128 + 128] = v0[at, :]
+        if c == 0:
+            pl.semaphore_wait(
+                barrier,
+                leaves - 1 + (lobe > 0).astype(jnp.int32) + (lobe < lobes - 1).astype(jnp.int32),
+            )
+        start_z(zs, zr, 0, 0, c)
+    send_links(v0, 0, low_faces(v0))
     loads[2].wait()
     loads[3].wait()
     loads[4].wait()
@@ -439,7 +464,6 @@
     lax.fori_loop(0, 8, grad_two, 0, unroll=2)
     advance(v0, v1, 0)
 
-    send_faces(v1, 1)
     scale_square = (1.0 / size[...]) ** 2
 
     def recip_body(b, carry):
@@ -467,7 +491,7 @@
         put_across(res, 0, j, dot(table[ROW_IK : ROW_IK + 64, :192], stack(across(v2, 0, j))))
         return carry
 
-    lax.fori_loop(0, 8, div_one, 0, unroll=4)
+    lax.fori_loop(0, 8, div_one, 0, unroll=8)
 
     def div_two(i, carry):
         both = jnp.concatenate([stack(ld(v2, spot(1, i), 64)), stack(ld(v2, spot(2, i), 64))], axis=0)
@@ -475,15 +499,16 @@
         st(res, spot(0, i), scale * (ld(res, spot(0, i), 64) + y))
         return carry
 
-    lax.fori_loop(0, 8, div_two, 0, unroll=4)
-    for side, k in ((0, 0), (1, 7)):
-        for h, at in enumerate(ends_of(res, 0, k)):
-            zs1[0, side, :, h * 128 : h * 128 + 128] = res[at, :]
-    start_z(zs1, zr1, 0, 2)
+    lax.fori_loop(0, 8, div_two, 0, unroll=8)
     face2 = jnp.concatenate([ld(res, i * 64, 8) for i in range(8)], axis=0)
     face3 = jnp.concatenate([ld(res, i * 64 + 56, 8) for i in range(8)], axis=0)
-    fill_message(2, face2, face3, [res[0:64, :]], [res[512 + 448 : 512 + 512, :]])
+    nothing = jnp.zeros((rows, 128), F32)
+    fill_message(2, nothing, face2, face3, [res[0:64, :]], [res[512 + 448 : 512 + 512, :]])
     start_links(2)
+    for f, k in ((0, 0), (1, 7)):
+        for h, at in enumerate(ends_of(res, 0, k)):
+            zs1[0, f, :, h * 128 : h * 128 + 128] = res[at, :]
+    start_z(zs1, zr1, 0, 2, 0)
 
     def forward(i, carry):
         y = dot(table[ROW_INT : ROW_INT + MODES16, :192], stack(ld(res, spot(0, i), 64)))
@@ -499,7 +524,7 @@
     for n, plane in ((0, near0), (9, near1)):
         y = dot(table[ROW_INT : ROW_INT + MODES16, :192], stack(plane))
         modes[n * MODES : (n + 1) * MODES, :] = y[:MODES]
-    wait_z(zs1, zr1, 0, 2, False)
+    wait_z(zs1, zr1, 0, 2, 0, False)
     for i in range(8):
         r0 = slice(i * 8, i * 8 + 8)
         layer = jnp.concatenate(
@@ -547,12 +572,13 @@
         zs1[1, 1, pl.ds(r0, 8), :] = y[88:96]
         return carry
 
-    lax.fori_loop(0, 8, backward, 0, unroll=4)
-    start_z(zs1, zr1, 1, 3)
+    lax.fori_loop(0, 8, backward, 0, unroll=8)
     fill_message(
-        3, outer[128:192, :], outer[192:256, :], [outer[0:64, 0:128]], [outer[64:128, 128:256]]
+        3, nothing, outer[128:192, :], outer[192:256, :],
+        [outer[0:64, 0:128]], [outer[64:128, 128:256]],
     )
     start_links(3)
+    start_z(zs1, zr1, 1, 3, 0)
     near0, near1 = chain_near(outer[0:64, :], outer[64:128, :])
     wait_links(3, False)
     near, ends = read_links(3, 1)
@@ -562,10 +588,10 @@
         for f, j in ((0, 0), (1, 7)):
             at = i * 64 + j * 8
             add(press, at, near[i * 8 : i * 8 + 8, f * EL : (f + 1) * EL])
-    wait_z(zs1, zr1, 1, 3, False)
-    for side, k in ((0, 0), (1, 7)):
+    wait_z(zs1, zr1, 1, 3, 0, False)
+    for f, k in ((0, 0), (1, 7)):
         for h, at in enumerate(ends_of(press, 0, k)):
-            press[at, :] = press[at, :] + zr1[1, side, :, h * 128 : h * 128 + 128]
+            press[at, :] = press[at, :] + zr1[1, f, :, h * 128 : h * 128 + 128]
     press_copies = [
         pltpu.make_async_copy(press.at[h * 512 : h * 512 + 512], press_hbm.at[:, h * 128 : h * 128 + 128], out_sem.at[2 + h])
         for h in range(2)
@@ -575,10 +601,23 @@
     for x in range(4):
         wait_links(x, True)
         if x < 2:
-            wait_z(zs, zr, x, x, True)
+            for c in range(3):
+                wait_z(zs, zr, x, x, c, True)
         else:
-            wait_z(zs1, zr1, x - 2, x, True)
+            wait_z(zs1, zr1, x - 2, x, 0, True)
     for copy in out_copies + press_copies:
+        copy.wait()
+
+
+def hand_over(first, second, first_out, second_out, sem):
+    copies = []
+    for q in range(PIECES):
+        at = pl.ds(q * (1536 // PIECES), 1536 // PIECES)
+        copies.append(pltpu.make_async_copy(first.at[at], first_out.at[at], sem.at[q]))
+    copies.append(pltpu.make_async_copy(second, second_out, sem.at[PIECES]))
+    for copy in copies:
+        copy.start()
+    for copy in copies:
         copy.wait()
 
 
@@ -614,8 +653,8 @@
         pltpu.VMEM((rows, 768), BF16),
         pltpu.SemaphoreType.DMA((7,)),
         pltpu.SemaphoreType.DMA((4,)),
-        pltpu.SemaphoreType.DMA((4, 2)),
-        pltpu.SemaphoreType.DMA((4, 2)),
+        pltpu.SemaphoreType.DMA((4, 2, 3)),
+        pltpu.SemaphoreType.DMA((4, 2, 3)),
         pltpu.SemaphoreType.DMA((4,)),
         pltpu.SemaphoreType.DMA((4,)),
     ]
@@ -632,13 +671,29 @@
             collective_id=0, has_side_effects=True, vmem_limit_bytes=40 * 1024 * 1024
         ),
     )(
-        base_velocity.reshape(1536, EL),
-        adjoint_velocity.reshape(1536, EL),
-        element_size.reshape(1, EL),
-        link_slot.reshape(1, leaves * 4),
-        jnp.asarray(table),
-        jnp.asarray(sums),
+        *[
+            pltpu.with_memory_space_constraint(one, pltpu.HBM)
+            for one in (
+                base_velocity.reshape(1536, EL),
+                adjoint_velocity.reshape(1536, EL),
+                element_size.reshape(1, EL),
+                link_slot.reshape(1, leaves * 4),
+                jnp.asarray(table),
+                jnp.asarray(sums),
+            )
+        ]
     )
+    out, press = pl.pallas_call(
+        hand_over,
+        out_shape=(
+            pltpu.HBM((1536, EL), F32),
+            pltpu.HBM((512, EL), F32),
+        ),
+        in_specs=[any_space] * 2,
+        out_specs=(any_space, any_space),
+        scratch_shapes=[pltpu.SemaphoreType.DMA((PIECES + 1,))],
+        compiler_params=pltpu.CompilerParams(vmem_limit_bytes=32 * 1024 * 1024),
+    )(out, press)
     return out.reshape(3, 512, EL), press
 
 

time: 45.7 us -> 37.2 us (0.81)
  local copies, waits for them, and re-layouts: 7.93 us -> 0 us
    unnamed x14 -> x0, local copies, waits for them, and re-layouts: 7.93 us -> none
    pallas_call x1, Pallas kernels: 36.6 us -> 35.1 us  [local(): pl.pallas_call(functools.partial(kernel, leaves, lobes), out_shape=(jax.S...]
    pallas_call x0 -> x1, Pallas kernels: none -> 1.35 us  [local(): pl.pallas_call(hand_over, out_shape=(pltpu.HBM((1536, EL), F32), pltpu.HB...]
where the time goes in v1:
time: 37.2 us; the launch traced here: 37.1 us
  Pallas kernels  36.5 us (98%)
  between operations  0.64 us (2%)
    pallas_call x1, Pallas kernels, local(): pl.pallas_call(functools.partial(kernel, leaves, lobes), out_shape=(jax.S...  35.1 us
    pallas_call x1, Pallas kernels, local(): pl.pallas_call(hand_over, out_shape=(pltpu.HBM((1536, EL), F32), pltpu.HB...  1.35 us

profile of v1, /device:TPU:97, one launch (start us, length us, event | category | flops | bytes accessed | tf_op | source)
XLA Modules:
  0.0 37.1 jit_solution(512010474683662986)
XLA Ops:
  0.6 35.1 %shard_map.77 = (f32[1536,256]{1,0:T(8,128)S(1)}, f32[512,256]{1,0:T(8,128)S(1)}) custom-call(f32[1536,256]{1,0:T(8,128)} %bitcast.5, f32[1536,256]{1,0:T(8,128)} %bitcast.6, f32[1,256]{1,0:T(1,128)} %bitcast.7, s32[1,128]{1,0:T(1,128)} %bitcast.8, bf16[704,384]{1,0:T(8,128)(2,1)} %constant.4.clone.table_hbm, f32[104,128]{1,0:T(8,128)} %constant.5.clone.sums_hbm), custom_call_target="tpu_custom_call" | custom-call | tf_op jit(solution)/shard_map/pallas_call | solution.py:661
  35.8 1.3 %shard_map.78 = (f32[1536,256]{1,0:T(8,128)}, f32[512,256]{1,0:T(8,128)}) custom-call(f32[1536,256]{1,0:T(8,128)S(1)} %get-tuple-element.6.first, f32[512,256]{1,0:T(8,128)S(1)} %get-tuple-element.7.second), custom_call_target="tpu_custom_call" | custom-call | tf_op jit(solution)/shard_map/pallas_call | solution.py:686

commit v2 on v1

--- a/solution.py
+++ b/solution.py
@@ -10,7 +10,7 @@
 from jax.sharding import PartitionSpec as P
 
 NP = 8
-PIECES = 3
+PIECES = 1
 EL = 256
 MODES = 104
 MODES16 = 112
@@ -74,7 +74,8 @@
 
 
 WIDE = 384
-ROW_JK, ROW_IK, ROW_DIV, ROW_INT, ROW_LAY, ROW_BACK, ROW_END = 0, 192, 320, 384, 496, 608, 704
+ROW_JK, ROW_IK, ROW_DIV, ROW_INT, ROW_LAY, ROW_BACK = 0, 192, 320, 384, 496, 608
+ROW_ALONG, ROW_FIX, ROW_END = 704, 784, 848
 
 
 def constant_tables():
@@ -89,6 +90,13 @@
     table[ROW_JK : ROW_JK + 192, :192] = three(plane)
     table[ROW_IK : ROW_IK + 128, :192] = three(along)
     table[ROW_DIV : ROW_DIV + 64, :384] = np.concatenate([three(first), three(second)], axis=1)
+    points = np.arange(64).reshape(8, 8)
+    shell = np.concatenate([points[0], points[7], points[:, 0], points[:, 7]])
+    put = np.zeros((64, 32))
+    put[shell, np.arange(32)] = 1.0
+    fix = np.concatenate([first @ put, second @ put], axis=1)
+    table[ROW_FIX : ROW_FIX + 64, :192] = three(fix)
+    table[ROW_FIX : ROW_FIX + 64, 192:256] = np.concatenate([put, put], axis=1)
     both = np.kron(sine, sine)
     grid = np.arange(100).reshape(10, 10)
     inner = grid[1:9, 1:9].reshape(-1)
@@ -100,6 +108,7 @@
     backward = np.zeros((96, MODES16))
     backward[:, :100] = both[np.concatenate([inner, layers])]
     table[ROW_BACK : ROW_BACK + 96, : 3 * MODES16] = three(backward)
+    table[ROW_ALONG : ROW_ALONG + 80, :240] = three(np.kron(sine, one))
     sums = np.zeros((MODES,))
     sums[:100] = (eigen[:, None] + eigen[None, :]).reshape(-1)
     sums = np.tile(sums[:, None], (1, 128)).astype(np.float32)
@@ -110,6 +119,10 @@
     high = x.astype(BF16)
     low = (x - high.astype(F32)).astype(BF16)
     return high, low
+
+
+def both_parts(x):
+    return jnp.concatenate(split(x), axis=1)
 
 
 def stack(x):
@@ -164,13 +177,13 @@
     out_hbm, press_hbm,
     base, v0, v1, v2, grads, part, res, modes, recip, press, outer,
     size, slot, table, sums,
-    zs, zr, zs1, zr1, msg, recv, a_lo, a_hi, chain_out, chain_in,
+    zs, zr, zs1, zr1, msg, recv, a_low, a_high, r_low, r_high, chain_in,
     in_sem, out_sem, z_send, z_recv, l_send, l_recv,
 ):
     me = lax.axis_index("leaf")
     lobe = lax.axis_index("lobe")
     rows = leaves * 8
-    sine, eigen = schwarz_tables()
+    eigen = schwarz_tables()[1]
 
     barrier = pltpu.get_barrier_semaphore()
     peers = far_first(me, leaves)
@@ -191,14 +204,18 @@
             barrier, inc=1, device_id={"lobe": lobe + 1}, device_id_type=pl.DeviceIdType.MESH
         )
 
-    loads = [
-        pltpu.make_async_copy(slot_hbm, slot, in_sem.at[0]),
-        pltpu.make_async_copy(adj_hbm.at[:, 0:128], v0.at[0:1536], in_sem.at[1]),
-        pltpu.make_async_copy(table_hbm, table, in_sem.at[2]),
-        pltpu.make_async_copy(size_hbm, size, in_sem.at[3]),
-        pltpu.make_async_copy(base_hbm, base, in_sem.at[4]),
-        pltpu.make_async_copy(sums_hbm, sums, in_sem.at[5]),
-        pltpu.make_async_copy(adj_hbm.at[:, 128:256], v0.at[1536:3072], in_sem.at[6]),
+    loads = [pltpu.make_async_copy(slot_hbm, slot, in_sem.at[0])]
+    for c in range(3):
+        for h in range(2):
+            loads.append(pltpu.make_async_copy(
+                adj_hbm.at[c * 512 : c * 512 + 512, h * 128 : h * 128 + 128],
+                v0.at[h * 1536 + c * 512 : h * 1536 + c * 512 + 512], in_sem.at[1 + c * 2 + h],
+            ))
+    loads += [
+        pltpu.make_async_copy(table_hbm, table, in_sem.at[7]),
+        pltpu.make_async_copy(size_hbm, size, in_sem.at[8]),
+        pltpu.make_async_copy(base_hbm, base, in_sem.at[9]),
+        pltpu.make_async_copy(sums_hbm, sums, in_sem.at[10]),
     ]
     for load in loads:
         load.start()
@@ -223,18 +240,27 @@
     spread = ((row >> 3) * 4 + (row & 3) == col).astype(F32)
     all_hot = dot_nt(spread.astype(BF16), hot.astype(BF16))
     low_row = (lax.broadcasted_iota(jnp.int32, (rows, 512), 0) & 4) == 0
-    a_lo[...] = jnp.where(low_row, all_hot, 0.0).astype(BF16)
-    a_hi[...] = jnp.where(low_row, 0.0, all_hot).astype(BF16)
+    low_hot = jnp.where(low_row, all_hot, 0.0).astype(BF16)
+    high_hot = jnp.where(low_row, 0.0, all_hot).astype(BF16)
+    for part_at in range(2):
+        a_low[:, part_at * 512 : part_at * 512 + 512] = low_hot
+        a_high[:, part_at * 512 : part_at * 512 + 512] = high_hot
+        r_low[part_at * rows : part_at * rows + rows, :] = low_hot
+        r_high[part_at * rows : part_at * rows + rows, :] = high_hot
     for cc in range(3):
         row = lax.broadcasted_iota(jnp.int32, (rows, 128), 0)
         col = lax.broadcasted_iota(jnp.int32, (rows, 128), 1)
         after, before = (me + 1) * 8 + 4 + cc, (me - 1) * 8 + 4 + cc
         pick = ((row == after) & (col == 127)) | ((row == before) & (col == 0))
-        chain_out[:, cc * 128 : cc * 128 + 128] = pick.astype(F32).astype(BF16)
+        pick = pick.astype(F32).astype(BF16)
+        a_high[:, 1024 + cc * 256 : 1024 + cc * 256 + 128] = pick
+        a_high[:, 1024 + cc * 256 + 128 : 1024 + cc * 256 + 256] = pick
         row = lax.broadcasted_iota(jnp.int32, (rows, EL), 0)
         col = lax.broadcasted_iota(jnp.int32, (rows, EL), 1)
         put = ((row == before) & (col == 0)) | ((row == after) & (col == EL - 1))
-        chain_in[:, cc * EL : (cc + 1) * EL] = put.astype(F32).astype(BF16)
+        put = put.astype(F32).astype(BF16)
+        chain_in[0:rows, cc * EL : (cc + 1) * EL] = put
+        chain_in[rows : 2 * rows, cc * EL : (cc + 1) * EL] = put
 
     def z_copies(sends, recvs, at, x, c):
         rows_of = pl.ds(c * 64, 64)
@@ -289,41 +315,34 @@
         )
         copy.wait_send() if sent else copy.wait_recv()
 
-    def zeros64(width):
-        return jnp.zeros((64, width), F32)
-
     def low_message(face2, face3):
-        total = jnp.zeros((rows, 128), F32)
-        for f, face in enumerate((face2, face3)):
-            for piece in split(face):
-                total += dot_nt(a_lo[:, f * EL : (f + 1) * EL], piece)
-        return total
+        return dot_nt(a_low[...], both_parts(jnp.concatenate([face2, face3], axis=1)))
 
     def fill_message(x, total, face2, face3, leads, tails):
         end_lane = lax.broadcasted_iota(jnp.int32, (64, 128), 1)
-        for f, face in enumerate((face2, face3)):
-            for piece in split(jnp.concatenate([face, zeros64(EL)], axis=0)):
-                total += dot_nt(a_hi[:, f * EL : (f + 1) * EL], piece)
-        for cc in range(len(leads)):
-            ends = jnp.where(
-                end_lane == 0, leads[cc], jnp.where(end_lane == 127, tails[cc], 0.0)
-            )
-            ends = jnp.concatenate([zeros64(128), ends], axis=0)
-            for piece in split(ends):
-                total += dot_nt(chain_out[:, cc * 128 : (cc + 1) * 128], piece)
-        msg[x] = total
+        ends = [
+            jnp.where(end_lane == 0, lead, jnp.where(end_lane == 127, tail, 0.0))
+            for lead, tail in zip(leads, tails)
+        ]
+        faces = both_parts(jnp.concatenate([face2, face3], axis=1))
+        ends = jnp.concatenate([both_parts(one) for one in ends], axis=1)
+        width = ends.shape[1]
+        right = jnp.concatenate(
+            [
+                jnp.concatenate([faces, jnp.zeros((64, width), BF16)], axis=1),
+                jnp.concatenate([jnp.zeros((64, 1024), BF16), ends], axis=1),
+            ],
+            axis=0,
+        )
+        high = dot_nt(a_high[:, : 1024 + width], right)
+        msg[x] = high if total is None else total + high
 
     def read_links(x, count):
-        turned = jnp.transpose(recv[x])
-        high, low = split(turned)
-        near = []
+        parts = both_parts(jnp.transpose(recv[x]))
+        near = dot(parts[:64], r_high[...])
         if count == 3:
-            near.append(dot(high, a_lo[...]) + dot(low, a_lo[...]))
-        near.append((dot(high, a_hi[...]) + dot(low, a_hi[...]))[:64])
-        near = jnp.concatenate(near, axis=0) if count == 3 else near[0]
-        wide = count * EL
-        ends = dot(high[64:], chain_in[:, :wide]) + dot(low[64:], chain_in[:, :wide])
-        return near, ends
+            near = jnp.concatenate([dot(parts, r_low[...]), near], axis=0)
+        return near, dot(parts[64:], chain_in[:, : count * EL])
 
     def spot(c, i):
         return pl.multiple_of(c * 512 + i * 64, 64)
@@ -364,9 +383,16 @@
         leads = [v[c * 512 : c * 512 + 64, :] for c in range(3)]
         tails = [v[1536 + c * 512 + 448 : 1536 + c * 512 + 512, :] for c in range(3)]
         fill_message(x, total, side(v, (2,), 0), side(v, (2,), 7), leads, tails)
+        if x == 0:
+            pl.semaphore_wait(
+                barrier,
+                leaves - 1 + (lobe > 0).astype(jnp.int32) + (lobe < lobes - 1).astype(jnp.int32),
+            )
+            for c in range(3):
+                start_z(zs, zr, 0, 0, c)
         start_links(x)
 
-    def advance(v, w, x):
+    def advance(v, w):
         scale = 2.0 / size[...]
         visc = viscosity * scale
         step = time_step * scale
@@ -400,51 +426,37 @@
             near0, near1 = chain_near(ld(v, spot(c, 0), 64), ld(v, spot(c, 7), 64))
             add(w, spot(c, 0), penalty * near0)
             add(w, spot(c, 7), penalty * near1)
-        wait_links(x, False)
-        near, ends = read_links(x, 3)
+    def add_links(w, near, ends):
         for c in range(3):
             end = ends[:, c * EL : (c + 1) * EL]
             add(w, spot(c, 0), jnp.where(lane == 0, penalty * end, 0.0))
             add(w, spot(c, 7), jnp.where(lane == EL - 1, penalty * end, 0.0))
             for i in range(8):
                 for f, j in ((0, 0), (1, 7)):
-                    at = c * 512 + i * 64 + j * 8
                     r0 = c * 64 + i * 8
-                    add(w, at, penalty * near[r0 : r0 + 8, f * EL : (f + 1) * EL])
-        total = None
-        for c in range(3):
-            wait_z(zs, zr, x, x, c, False)
-            for f, k in ((0, 0), (1, 7)):
-                for h, at in enumerate(ends_of(w, c * 512, k)):
-                    here = slice(c * 64, c * 64 + 64), slice(h * 128, h * 128 + 128)
-                    value = w[at, :] + penalty * zr[x, f, here[0], here[1]]
-                    w[at, :] = value
-                    if x == 0:
-                        zs[1, f, here[0], here[1]] = value
-            if x == 0:
-                start_z(zs, zr, 1, 1, c)
-                if c == 1:
-                    total = low_faces(w)
-        if x == 0:
-            send_links(w, 1, total)
-
-    loads[1].wait()
-    loads[6].wait()
+                    add(
+                        w, c * 512 + i * 64 + j * 8,
+                        penalty * near[r0 : r0 + 8, f * EL : (f + 1) * EL],
+                    )
+
+    def add_z(w, x, c):
+        for f, k in ((0, 0), (1, 7)):
+            for h, at in enumerate(ends_of(w, c * 512, k)):
+                here = slice(c * 64, c * 64 + 64), slice(h * 128, h * 128 + 128)
+                value = w[at, :] + penalty * zr[x, f, here[0], here[1]]
+                w[at, :] = value
+                if x == 0:
+                    zs[1, f, here[0], here[1]] = value
+
     for c in range(3):
+        loads[1 + 2 * c].wait()
+        loads[2 + 2 * c].wait()
         for f, k in ((0, 0), (1, 7)):
             for h, at in enumerate(ends_of(v0, c * 512, k)):
                 zs[0, f, c * 64 : c * 64 + 64, h * 128 : h * 128 + 128] = v0[at, :]
-        if c == 0:
-            pl.semaphore_wait(
-                barrier,
-                leaves - 1 + (lobe > 0).astype(jnp.int32) + (lobe < lobes - 1).astype(jnp.int32),
-            )
-        start_z(zs, zr, 0, 0, c)
     send_links(v0, 0, low_faces(v0))
-    loads[2].wait()
-    loads[3].wait()
-    loads[4].wait()
-    loads[5].wait()
+    for load in loads[7:]:
+        load.wait()
 
     def grad_one(j, carry):
         for r in range(3):
@@ -462,7 +474,17 @@
         return carry
 
     lax.fori_loop(0, 8, grad_two, 0, unroll=2)
-    advance(v0, v1, 0)
+    advance(v0, v1)
+    wait_links(0, False)
+    add_links(v1, *read_links(0, 3))
+    total = None
+    for c in range(3):
+        wait_z(zs, zr, 0, 0, c, False)
+        add_z(v1, 0, c)
+        start_z(zs, zr, 1, 1, c)
+        if c == 1:
+            total = low_faces(v1)
+    send_links(v1, 1, total)
 
     scale_square = (1.0 / size[...]) ** 2
 
@@ -477,13 +499,7 @@
         return carry
 
     lax.fori_loop(0, MODES // 8, recip_body, 0)
-    advance(v1, v2, 1)
-    out_copies = [
-        pltpu.make_async_copy(v2.at[h * 1536 : h * 1536 + 1536], out_hbm.at[:, h * 128 : h * 128 + 128], out_sem.at[h])
-        for h in range(2)
-    ]
-    for copy in out_copies:
-        copy.start()
+    advance(v1, v2)
 
     scale = 2.0 / size[...]
 
@@ -491,24 +507,68 @@
         put_across(res, 0, j, dot(table[ROW_IK : ROW_IK + 64, :192], stack(across(v2, 0, j))))
         return carry
 
-    lax.fori_loop(0, 8, div_one, 0, unroll=8)
+    lax.fori_loop(0, 8, div_one, 0, unroll=4)
+
+    def div_pair(first_part, second_part):
+        both = jnp.concatenate([stack(first_part), stack(second_part)], axis=0)
+        return dot(table[ROW_DIV : ROW_DIV + 64, :], both)
 
     def div_two(i, carry):
-        both = jnp.concatenate([stack(ld(v2, spot(1, i), 64)), stack(ld(v2, spot(2, i), 64))], axis=0)
-        y = dot(table[ROW_DIV : ROW_DIV + 64, :], both)
-        st(res, spot(0, i), scale * (ld(res, spot(0, i), 64) + y))
+        add(res, spot(0, i), div_pair(ld(v2, spot(1, i), 64), ld(v2, spot(2, i), 64)))
         return carry
 
-    lax.fori_loop(0, 8, div_two, 0, unroll=8)
+    lax.fori_loop(0, 8, div_two, 0, unroll=4)
+
+    wait_links(1, False)
+    near, ends = read_links(1, 3)
+    end0 = [jnp.where(lane == 0, penalty * ends[:, c * EL : (c + 1) * EL], 0.0) for c in range(3)]
+    end1 = [
+        jnp.where(lane == EL - 1, penalty * ends[:, c * EL : (c + 1) * EL], 0.0) for c in range(3)
+    ]
+    ends_fix = {0: div_pair(end0[1], end0[2]), 7: div_pair(end1[1], end1[2])}
+    for c in range(3):
+        wait_z(zs, zr, 1, 1, c, False)
+
+    def shell(c, f):
+        here = slice(c * 64, c * 64 + 64)
+        if f < 2:
+            return penalty * near[here, f * EL : (f + 1) * EL]
+        return penalty * zr[1, f - 2, here, :]
+
+    shells = [[shell(c, f) for f in range(4)] for c in range(3)]
+    along_i = [dot(table[ROW_IK : ROW_IK + 64, :192], stack(one)) for one in shells[0]]
+    diff = node_tables()
+    for i in range(8):
+        r0 = slice(i * 8, i * 8 + 8)
+        plane = jnp.concatenate([shells[c][f][r0] for c in (1, 2) for f in range(4)], axis=0)
+        rest = split(jnp.concatenate([one[r0] for one in along_i], axis=0))
+        y = dot(
+            table[ROW_FIX : ROW_FIX + 64, :256], jnp.concatenate([stack(plane), *rest], axis=0)
+        )
+        y += float(diff[i, 0]) * end0[0] + float(diff[i, 7]) * end1[0]
+        if i in ends_fix:
+            y += ends_fix[i]
+        st(res, i * 64, scale * (ld(res, i * 64, 64) + y))
     face2 = jnp.concatenate([ld(res, i * 64, 8) for i in range(8)], axis=0)
     face3 = jnp.concatenate([ld(res, i * 64 + 56, 8) for i in range(8)], axis=0)
-    nothing = jnp.zeros((rows, 128), F32)
-    fill_message(2, nothing, face2, face3, [res[0:64, :]], [res[512 + 448 : 512 + 512, :]])
+    fill_message(2, None, face2, face3, [res[0:64, :]], [res[512 + 448 : 512 + 512, :]])
     start_links(2)
     for f, k in ((0, 0), (1, 7)):
         for h, at in enumerate(ends_of(res, 0, k)):
             zs1[0, f, :, h * 128 : h * 128 + 128] = res[at, :]
     start_z(zs1, zr1, 0, 2, 0)
+
+    add_links(v2, near, ends)
+    for c in range(3):
+        add_z(v2, 1, c)
+    out_copies = [
+        pltpu.make_async_copy(
+            v2.at[h * 1536 : h * 1536 + 1536], out_hbm.at[:, h * 128 : h * 128 + 128], out_sem.at[h]
+        )
+        for h in range(2)
+    ]
+    for copy in out_copies:
+        copy.start()
 
     def forward(i, carry):
         y = dot(table[ROW_INT : ROW_INT + MODES16, :192], stack(ld(res, spot(0, i), 64)))
@@ -533,52 +593,47 @@
         y = dot(table[ROW_LAY : ROW_LAY + MODES16, :96], stack(layer))
         modes[(i + 1) * MODES : (i + 2) * MODES, :] += y[:MODES]
 
-    def along(values):
-        plus = [values[n] + values[9 - n] for n in range(5)]
-        minus = [values[n] - values[9 - n] for n in range(5)]
-        result = []
-        for m in range(10):
-            terms = plus if m % 2 == 0 else minus
-            total = terms[0] * float(np.float32(sine[m, 0]))
-            for n in range(1, 5):
-                total += terms[n] * float(np.float32(sine[m, n]))
-            result.append(total)
-        return result
+    along = table[ROW_ALONG : ROW_ALONG + 80, :240]
 
     def solve(b, carry):
         at = [pl.ds(pl.multiple_of(m * MODES + b * 8, 8), 8) for m in range(10)]
-        values = along([modes[at[m], :] for m in range(10)])
-        values = along([values[m] * recip[at[m], :] for m in range(10)])
+        values = jnp.concatenate([modes[one, :] for one in at], axis=0)
+        values = dot(along, stack(values))
+        values = values * jnp.concatenate([recip[one, :] for one in at], axis=0)
+        values = dot(along, stack(values))
         for m in range(10):
-            modes[at[m], :] = values[m]
+            modes[at[m], :] = values[m * 8 : m * 8 + 8]
         return carry
 
-    lax.fori_loop(0, MODES // 8, solve, 0)
+    lax.fori_loop(0, MODES // 8, solve, 0, unroll=MODES // 8)
 
     pad = jnp.zeros((MODES16 - MODES, EL), F32)
+
+    def mode_plane(n):
+        plane = modes[pl.ds(pl.multiple_of(n * MODES, 8), MODES), :]
+        return stack(jnp.concatenate([plane, pad], axis=0))
+
+    for i in range(8):
+        y = dot(table[ROW_BACK + 64 : ROW_BACK + 96, : 3 * MODES16], mode_plane(i + 1))
+        r0 = slice(i * 8, i * 8 + 8)
+        outer[128 + i * 8 : 136 + i * 8, :] = y[0:8]
+        outer[192 + i * 8 : 200 + i * 8, :] = y[8:16]
+        zs1[1, 0, r0, :] = y[16:24]
+        zs1[1, 1, r0, :] = y[24:32]
     for n, at in ((0, 0), (9, 64)):
-        plane = jnp.concatenate([modes[n * MODES : (n + 1) * MODES, :], pad], axis=0)
-        outer[at : at + 64, :] = dot(table[ROW_BACK : ROW_BACK + 64, : 3 * MODES16], stack(plane))
-
-    def backward(i, carry):
-        plane = modes[pl.ds(pl.multiple_of((i + 1) * MODES, 8), MODES), :]
-        plane = jnp.concatenate([plane, pad], axis=0)
-        y = dot(table[ROW_BACK : ROW_BACK + 96, : 3 * MODES16], stack(plane))
-        st(press, spot(0, i), y[:64])
-        r0 = pl.multiple_of(i * 8, 8)
-        outer[pl.ds(128 + r0, 8), :] = y[64:72]
-        outer[pl.ds(192 + r0, 8), :] = y[72:80]
-        zs1[1, 0, pl.ds(r0, 8), :] = y[80:88]
-        zs1[1, 1, pl.ds(r0, 8), :] = y[88:96]
-        return carry
-
-    lax.fori_loop(0, 8, backward, 0, unroll=8)
+        outer[at : at + 64, :] = dot(table[ROW_BACK : ROW_BACK + 64, : 3 * MODES16], mode_plane(n))
     fill_message(
-        3, nothing, outer[128:192, :], outer[192:256, :],
+        3, None, outer[128:192, :], outer[192:256, :],
         [outer[0:64, 0:128]], [outer[64:128, 128:256]],
     )
     start_links(3)
     start_z(zs1, zr1, 1, 3, 0)
+
+    def backward(i, carry):
+        st(press, spot(0, i), dot(table[ROW_BACK : ROW_BACK + 64, : 3 * MODES16], mode_plane(i + 1)))
+        return carry
+
+    lax.fori_loop(0, 8, backward, 0, unroll=4)
     near0, near1 = chain_near(outer[0:64, :], outer[64:128, :])
     wait_links(3, False)
     near, ends = read_links(3, 1)
@@ -589,15 +644,16 @@
             at = i * 64 + j * 8
             add(press, at, near[i * 8 : i * 8 + 8, f * EL : (f + 1) * EL])
     wait_z(zs1, zr1, 1, 3, 0, False)
-    for f, k in ((0, 0), (1, 7)):
-        for h, at in enumerate(ends_of(press, 0, k)):
+    press_copies = []
+    for h in range(2):
+        for f, k in ((0, 0), (1, 7)):
+            at = ends_of(press, 0, k)[h]
             press[at, :] = press[at, :] + zr1[1, f, :, h * 128 : h * 128 + 128]
-    press_copies = [
-        pltpu.make_async_copy(press.at[h * 512 : h * 512 + 512], press_hbm.at[:, h * 128 : h * 128 + 128], out_sem.at[2 + h])
-        for h in range(2)
-    ]
-    for copy in press_copies:
+        copy = pltpu.make_async_copy(
+            press.at[h * 512 : h * 512 + 512], press_hbm.at[:, h * 128 : h * 128 + 128], out_sem.at[2 + h]
+        )
         copy.start()
+        press_copies.append(copy)
     for x in range(4):
         wait_links(x, True)
         if x < 2:
@@ -647,11 +703,12 @@
         pltpu.VMEM((2, 2, 64, EL), F32),
         pltpu.VMEM((4, rows, 128), F32),
         pltpu.VMEM((4, rows, 128), F32),
-        pltpu.VMEM((rows, 512), BF16),
-        pltpu.VMEM((rows, 512), BF16),
-        pltpu.VMEM((rows, 384), BF16),
-        pltpu.VMEM((rows, 768), BF16),
-        pltpu.SemaphoreType.DMA((7,)),
+        pltpu.VMEM((rows, 1024), BF16),
+        pltpu.VMEM((rows, 1792), BF16),
+        pltpu.VMEM((2 * rows, 512), BF16),
+        pltpu.VMEM((2 * rows, 512), BF16),
+        pltpu.VMEM((2 * rows, 768), BF16),
+        pltpu.SemaphoreType.DMA((11,)),
         pltpu.SemaphoreType.DMA((4,)),
         pltpu.SemaphoreType.DMA((4, 2, 3)),
         pltpu.SemaphoreType.DMA((4, 2, 3)),

time: 37.2 us -> 35.8 us (0.962)
  Pallas kernels: 36.5 us -> 35.1 us
    pallas_call x1, Pallas kernels: 35.1 us -> 33.8 us  [local(): pl.pallas_call(functools.partial(kernel, leaves, lobes), out_shape=(jax.S...]
where the time goes in v2:
time: 35.8 us; the launch traced here: 35.7 us
  Pallas kernels  35.1 us (98%)
  between operations  0.64 us (2%)
    pallas_call x1, Pallas kernels, local(): pl.pallas_call(functools.partial(kernel, leaves, lobes), out_shape=(jax.S...  33.8 us
    pallas_call x1, Pallas kernels, local(): pl.pallas_call(hand_over, out_shape=(pltpu.HBM((1536, EL), F32), pltpu.HB...  1.33 us

profile of v2, /device:TPU:97, one launch (start us, length us, event | category | flops | bytes accessed | tf_op | source)
XLA Modules:
  0.0 35.7 jit_solution(2110349902359180675)
XLA Ops:
  0.6 33.8 %shard_map.77 = (f32[1536,256]{1,0:T(8,128)S(1)}, f32[512,256]{1,0:T(8,128)S(1)}) custom-call(f32[1536,256]{1,0:T(8,128)} %bitcast.5, f32[1536,256]{1,0:T(8,128)} %bitcast.6, f32[1,256]{1,0:T(1,128)} %bitcast.7, s32[1,128]{1,0:T(1,128)} %bitcast.8, bf16[848,384]{1,0:T(8,128)(2,1)} %constant.4.clone.table_hbm, f32[104,128]{1,0:T(8,128)} %constant.5.clone.sums_hbm), custom_call_target="tpu_custom_call" | custom-call | tf_op jit(solution)/shard_map/pallas_call | solution.py:718
  34.4 1.3 %shard_map.78 = (f32[1536,256]{1,0:T(8,128)}, f32[512,256]{1,0:T(8,128)}) custom-call(f32[1536,256]{1,0:T(8,128)S(1)} %get-tuple-element.6.first, f32[512,256]{1,0:T(8,128)S(1)} %get-tuple-element.7.second), custom_call_target="tpu_custom_call" | custom-call | tf_op jit(solution)/shard_map/pallas_call | solution.py:743

commit v3 on v2

--- a/solution.py
+++ b/solution.py
@@ -217,7 +217,7 @@
         pltpu.make_async_copy(base_hbm, base, in_sem.at[9]),
         pltpu.make_async_copy(sums_hbm, sums, in_sem.at[10]),
     ]
-    for load in loads:
+    for load in loads[:7]:
         load.start()
 
     for x in range(4):
@@ -403,7 +403,7 @@
                 put_across(part, c, j, across(base, 0, j) * y[:64] + visc * y[64:])
             return carry
 
-        lax.fori_loop(0, 8, one, 0, unroll=2)
+        lax.fori_loop(0, 8, one, 0, unroll=4)
         sub = lax.broadcasted_iota(jnp.int32, (64, EL), 0)
         k, j = sub & 7, sub >> 3
         edge = ((k == 0) | (k == 7)).astype(F32) + ((j == 0) | (j == 7)).astype(F32)
@@ -421,7 +421,7 @@
                 st(w, spot(c, i), keep * own[c] + step * total)
             return carry
 
-        lax.fori_loop(0, 8, two, 0, unroll=2)
+        lax.fori_loop(0, 8, two, 0, unroll=4)
         for c in range(3):
             near0, near1 = chain_near(ld(v, spot(c, 0), 64), ld(v, spot(c, 7), 64))
             add(w, spot(c, 0), penalty * near0)
@@ -454,6 +454,8 @@
         for f, k in ((0, 0), (1, 7)):
             for h, at in enumerate(ends_of(v0, c * 512, k)):
                 zs[0, f, c * 64 : c * 64 + 64, h * 128 : h * 128 + 128] = v0[at, :]
+    for load in loads[7:]:
+        load.start()
     send_links(v0, 0, low_faces(v0))
     for load in loads[7:]:
         load.wait()
@@ -464,7 +466,7 @@
             put_across(grads, r, j, y)
         return carry
 
-    lax.fori_loop(0, 8, grad_one, 0, unroll=2)
+    lax.fori_loop(0, 8, grad_one, 0, unroll=4)
 
     def grad_two(i, carry):
         for r in range(3):
@@ -473,7 +475,7 @@
             grads[block(6 + r, i), :] = y[64:]
         return carry
 
-    lax.fori_loop(0, 8, grad_two, 0, unroll=2)
+    lax.fori_loop(0, 8, grad_two, 0, unroll=4)
     advance(v0, v1)
     wait_links(0, False)
     add_links(v1, *read_links(0, 3))

time: 35.8 us -> 35.5 us (level)
  Pallas kernels: 35.1 us -> 34.7 us
    pallas_call x1, Pallas kernels: 33.8 us -> 33.4 us  [local(): pl.pallas_call(functools.partial(kernel, leaves, lobes), out_shape=(jax.S...]
where the time goes in v3:
time: 35.5 us; the launch traced here: 35.4 us
  Pallas kernels  34.7 us (98%)
  between operations  0.64 us (2%)
    pallas_call x1, Pallas kernels, local(): pl.pallas_call(functools.partial(kernel, leaves, lobes), out_shape=(jax.S...  33.4 us
    pallas_call x1, Pallas kernels, local(): pl.pallas_call(hand_over, out_shape=(pltpu.HBM((1536, EL), F32), pltpu.HB...  1.33 us

profile of v3, /device:TPU:97, one launch (start us, length us, event | category | flops | bytes accessed | tf_op | source)
XLA Modules:
  0.0 35.4 jit_solution(12095164990886903421)
XLA Ops:
  0.6 33.4 %shard_map.77 = (f32[1536,256]{1,0:T(8,128)S(1)}, f32[512,256]{1,0:T(8,128)S(1)}) custom-call(f32[1536,256]{1,0:T(8,128)} %bitcast.5, f32[1536,256]{1,0:T(8,128)} %bitcast.6, f32[1,256]{1,0:T(1,128)} %bitcast.7, s32[1,128]{1,0:T(1,128)} %bitcast.8, bf16[848,384]{1,0:T(8,128)(2,1)} %constant.4.clone.table_hbm, f32[104,128]{1,0:T(8,128)} %constant.5.clone.sums_hbm), custom_call_target="tpu_custom_call" | custom-call | tf_op jit(solution)/shard_map/pallas_call | solution.py:720
  34.0 1.3 %shard_map.78 = (f32[1536,256]{1,0:T(8,128)}, f32[512,256]{1,0:T(8,128)}) custom-call(f32[1536,256]{1,0:T(8,128)S(1)} %get-tuple-element.6.first, f32[512,256]{1,0:T(8,128)S(1)} %get-tuple-element.7.second), custom_call_target="tpu_custom_call" | custom-call | tf_op jit(solution)/shard_map/pallas_call | solution.py:745
